TPU v7x, 32 devices: a whole 2x2x4 slice. The times are simulated.
32 devices in a mesh: dp: 4 (over x, core), head: 2 (over y), hidden: 4 (over z).
Axes of the slice: x: 2, y: 2, z: 4, core: 2. Of those that a mesh axis runs over, the one named last changes fastest.
Arguments:
- tokens: bfloat16 [16, 512, 1024], P(('dp', 'hidden'), 'head'), may hold values from -6 to 6
- lengths: int32 [16, 1], P(('dp', 'hidden')), may hold values from 449 to 512, as said below
- norm_first: float32 [1024], replicated, may hold values from 0.5 to 1.5
- w_qkv: bfloat16 [1024, 3, 1024], P(None, None, 'head'), may hold values from -0.1875 to 0.1875
- w_feature: bfloat16 [2, 16, 64, 64], P(None, 'head'), may hold values from -1.5 to 1.5
- w_out: bfloat16 [1024, 1024], P('head'), may hold values from -2 to 2
- norm_second: float32 [1024], replicated, may hold values from 0.5 to 1.5
- w_up: bfloat16 [1024, 4096], P(None, 'hidden'), may hold values from -0.1875 to 0.1875
- w_down: bfloat16 [4096, 1024], P('hidden'), may hold values from -0.09375 to 0.09375
- cotangent: bfloat16 [16, 512, 1024], P(('dp', 'hidden'), 'head'), may hold values from -6 to 6
Outputs:
- block_out: bfloat16 [16, 512, 1024], P(('dp', 'hidden'), 'head')
- grad_tokens: float32 [16, 512, 1024], P(('dp', 'hidden'), 'head')
- grad_norm_first: float32 [1024], replicated
- grad_qkv: float32 [1024, 3, 1024], P(None, None, 'head')
- grad_feature: float32 [2, 16, 64, 64], P(None, 'head')
- grad_out: float32 [1024, 1024], P('head')
- grad_norm_second: float32 [1024], replicated
- grad_up: float32 [1024, 4096], P(None, 'hidden')
- grad_down: float32 [4096, 1024], P('hidden')
Inputs may be any that keep to these rules, and one draw needn't show every extreme that they name: `lengths`: each bin holds a single sequence, padded up to whole blocks of 64 tokens, that fills the 512 slots of its bin exactly. In every draw some bin holds a sequence of exactly 512 tokens.
All inputs are finite; a program needn't handle non-finite values.
Results may differ from a plain program's by a relative error of at most 0.019.
Values may be sent and summed in bfloat16 or wider, within the bound.
A program may use at most 192 MiB of HBM per device.

v0:
```python
import jax, jax.numpy as jnp
from jax import lax
from jax.experimental import pallas as pl
from jax.experimental.pallas import tpu as pltpu
from jax.sharding import PartitionSpec as P
BF=jnp.bfloat16; F32=jnp.float32
NT=(((1,),(1,)),((),()))
TN=(((0,),(0,)),((),()))
SB=256

def mm(a,b): return jnp.dot(a,b,preferred_element_type=F32)
def mm_nt(a,b): return lax.dot_general(a,b,NT,preferred_element_type=F32)
def mm_tn(a,b): return lax.dot_general(a,b,TN,preferred_element_type=F32)

def half_ones(width, size):
    r=lax.broadcasted_iota(jnp.int32,(width,width),0)//size
    c=lax.broadcasted_iota(jnp.int32,(width,width),1)//size
    return (r==c).astype(F32).astype(BF)

def first_half(shape, size):
    return lax.broadcasted_iota(jnp.int32,shape,1)%(2*size) < size

def half_sum(t, ones):
    hi=t.astype(BF); lo=(t-hi.astype(F32)).astype(BF)
    return mm(hi,ones)+mm(lo,ones)

def features(x, w2, ones, size):
    u=mm(x,w2)
    h0=first_half(u.shape,size)
    big=jnp.float32(3e38)
    def both(f, fill):
        return jnp.where(h0, f(jnp.where(h0,u,fill)), f(jnp.where(h0,fill,u)))
    top=both(lambda t: jnp.max(t,axis=1,keepdims=True), -big)
    low=both(lambda t: jnp.min(t,axis=1,keepdims=True), big)
    e=jnp.concatenate([jnp.exp(u-top),jnp.exp(low-u)],axis=1)
    s=mm(e.astype(BF),ones)
    return e/s

def halves(t, h0):
    z=jnp.zeros_like(t)
    return jnp.where(h0,t,z), jnp.where(h0,z,t)

def attend(fq, fk, v, size):
    n=fq.shape[0]
    h0=first_half(fq.shape,size)
    fqs=halves(fq,h0)
    hv=first_half(v.shape,size)
    one=jnp.ones(v.shape,BF)
    ve=halves(jnp.concatenate([v,one],axis=1),h0)
    outs=[]
    for r in range(0,n,SB):
        ext=r+SB
        keep=(lax.broadcasted_iota(jnp.int32,(SB,ext),0)+r)>=lax.broadcasted_iota(jnp.int32,(SB,ext),1)
        acc=None
        for s in range(2):
            sc=mm_nt(fqs[s][r:r+SB],fk[:ext])
            sc=jnp.where(keep,sc,0.0).astype(BF)
            t=mm(sc,ve[s][:ext])
            acc=t if acc is None else acc+t
        outs.append(acc)
    p=jnp.concatenate(outs,axis=0)
    w=v.shape[1]
    rden=1.0/p[:,w:]
    return p[:,:w]*rden, rden

def attend_back(fq,fk,v,mixed,rden,datt,ones,size):
    n,w=v.shape
    wide=(n,2*w)
    h0=first_half(wide,size)
    dn=(datt*rden).astype(BF)
    dd=-half_sum(datt*mixed.astype(F32),ones)*rden
    hi=dd.astype(BF); lo=(dd-hi.astype(F32)).astype(BF)
    lane=lax.broadcasted_iota(jnp.int32,(n,w),1)%size
    zero=jnp.zeros((n,w),BF)
    ext_=jnp.where(lane==0,hi,jnp.where(lane==1,lo,zero))
    nx=halves(jnp.concatenate([dn,ext_],axis=1),h0)
    vx=jnp.concatenate([v,jnp.ones((n,w),BF)],axis=1)
    fqs=halves(fq,h0); fks=halves(fk,h0)
    dfq=[];dfk=[];dv=[]
    for r in range(0,n,SB):
        ext=r+SB
        keep=(lax.broadcasted_iota(jnp.int32,(SB,ext),0)+r)>=lax.broadcasted_iota(jnp.int32,(SB,ext),1)
        acc=0.0
        for s in range(2):
            ds=jnp.where(keep,mm_nt(nx[s][r:r+SB],vx[:ext]),0.0).astype(BF)
            acc=acc+mm(ds,fks[s][:ext])
        dfq.append(acc)
        left=n-r
        keep=lax.broadcasted_iota(jnp.int32,(SB,left),0)<=lax.broadcasted_iota(jnp.int32,(SB,left),1)
        ak=0.0; av=0.0
        for s in range(2):
            ds=jnp.where(keep,mm_nt(vx[r:r+SB],nx[s][r:]),0.0).astype(BF)
            ak=ak+mm(ds,fqs[s][r:])
            sc=jnp.where(keep,mm_nt(fk[r:r+SB],fqs[s][r:]),0.0).astype(BF)
            av=av+mm(sc,nx[s][r:,:w])
        dfk.append(ak); dv.append(av)
    cat=lambda t: jnp.concatenate(t,axis=0)
    return cat(dfq),cat(dfk),cat(dv)

def feature_back(f, df, ones):
    w=f.shape[1]//2
    f=f.astype(F32)
    part=f*(df-half_sum(f*df,ones))
    return (part[:,:w]-part[:,w:]).astype(BF)

def pair_weights(wf_ref, w2_ref):
    hd=wf_ref.shape[-1]
    w2_ref[...]=jnp.zeros_like(w2_ref)
    for t in range(2):
        for p in range(w2_ref.shape[1]):
            w2_ref[t,p,:hd,:hd]=wf_ref[t,2*p]
            w2_ref[t,p,hd:,hd:]=wf_ref[t,2*p+1]

def fwd_kernel(len_ref, rows_ref, wqkv_ref, wf_ref, wout_ref, proj_ref, feat_ref, mixed_ref, rden_ref, branch_ref, w2_ref):
    hd=wf_ref.shape[-1]; w=2*hd; n=rows_ref.shape[0]; pairs=w2_ref.shape[1]
    pair_weights(wf_ref,w2_ref)
    for i in range(3):
        proj_ref[i]=mm(rows_ref[...],wqkv_ref[i]).astype(BF)
    ones=half_ones(2*w,hd)
    valid=lax.broadcasted_iota(jnp.int32,(n,2*w),0)<len_ref[0,0]
    def body(p,_):
        c=pl.ds(pl.multiple_of(p*w,w),w)
        fq=features(proj_ref[0,:,c],w2_ref[0,p],ones,hd).astype(BF)
        fk=jnp.where(valid,features(proj_ref[1,:,c],w2_ref[1,p],ones,hd),0.0).astype(BF)
        feat_ref[0,p]=fq; feat_ref[1,p]=fk
        m,rd=attend(fq,fk,proj_ref[2,:,c],hd)
        mixed_ref[:,c]=m.astype(BF); rden_ref[:,c]=rd
        return 0
    lax.fori_loop(0,pairs,body,0)
    branch_ref[...]=mm(mixed_ref[...],wout_ref[...]).astype(branch_ref.dtype)

def bwd_kernel(rows_ref,wqkv_ref,wf_ref,wout_ref,proj_ref,feat_ref,mixed_ref,rden_ref,dbr_ref,
               gq_ref,gf_ref,go_ref,dfirst_ref,w2_ref,datt_ref,dproj_ref):
    hd=wf_ref.shape[-1]; w=2*hd; n=rows_ref.shape[0]; pairs=w2_ref.shape[1]
    pair_weights(wf_ref,w2_ref)
    ones=half_ones(2*w,hd); ones1=half_ones(w,hd)
    datt_ref[...]=mm_nt(dbr_ref[...],wout_ref[...])
    go_ref[...]=mm_tn(mixed_ref[...],dbr_ref[...]).astype(go_ref.dtype)
    def body(p,_):
        c=pl.ds(pl.multiple_of(p*w,w),w)
        fq=feat_ref[0,p]; fk=feat_ref[1,p]
        dfq,dfk,dv=attend_back(fq,fk,proj_ref[2,:,c],mixed_ref[:,c],rden_ref[:,c],datt_ref[:,c],ones1,hd)
        for t,(f,df) in enumerate(((fq,dfq),(fk,dfk))):
            du=feature_back(f,df,ones)
            g=mm_tn(proj_ref[t,:,c],du)
            gf_ref[t,2*p]=g[:hd,:hd].astype(gf_ref.dtype); gf_ref[t,2*p+1]=g[hd:,hd:].astype(gf_ref.dtype)
            dproj_ref[t,:,c]=mm_nt(du,w2_ref[t,p]).astype(BF)
        dproj_ref[2,:,c]=dv.astype(BF)
        return 0
    lax.fori_loop(0,pairs,body,0)
    acc=None
    for i in range(3):
        gq_ref[i]=mm_tn(rows_ref[...],dproj_ref[i]).astype(gq_ref.dtype)
        t=mm_nt(dproj_ref[i],wqkv_ref[i])
        acc=t if acc is None else acc+t
    dfirst_ref[...]=acc.astype(dfirst_ref.dtype)
VM=pl.BlockSpec(memory_space=pltpu.VMEM)
SM=pl.BlockSpec(memory_space=pltpu.SMEM)
S=jax.ShapeDtypeStruct
def fwd(length,rows,wqkv,wf,wout):
    n,d=rows.shape; c=wout.shape[0]; h=wf.shape[1]; hd=wf.shape[-1]
    return pl.pallas_call(fwd_kernel,
      out_shape=(S((3,n,c),BF),S((2,h//2,n,4*hd),BF),S((n,c),BF),S((n,c),F32),S((n,d),BF)),
      in_specs=[SM,VM,VM,VM,VM],out_specs=[VM]*5,
      scratch_shapes=[pltpu.VMEM((2,h//2,2*hd,2*hd),BF)],
      compiler_params=pltpu.CompilerParams(vmem_limit_bytes=56*2**20))(length,rows,wqkv,wf,wout)
def bwd(rows,wqkv,wf,wout,proj,feat,mixed,rden,dbr):
    n,d=rows.shape; c=wout.shape[0]; h=wf.shape[1]; hd=wf.shape[-1]
    return pl.pallas_call(bwd_kernel,
      out_shape=(S((3,d,c),BF),S((2,h,hd,hd),F32),S((c,d),BF),S((n,d),BF)),
      in_specs=[VM]*9,out_specs=[VM]*4,
      scratch_shapes=[pltpu.VMEM((2,h//2,2*hd,2*hd),BF),pltpu.VMEM((n,c),F32),pltpu.VMEM((3,n,c),BF)],
      compiler_params=pltpu.CompilerParams(vmem_limit_bytes=56*2**20))(rows,wqkv,wf,wout,proj,feat,mixed,rden,dbr)

EPS=1e-05

def normalize(values, gain):
    average = jnp.mean(values, axis=-1, keepdims=True)
    centred = values - average
    spread = jnp.mean(centred * centred, axis=-1, keepdims=True)
    return centred * lax.rsqrt(spread + EPS) * gain

def smooth_gate(values):
    return jax.nn.gelu(values, approximate=True)

def per_device(
    tokens, lengths, norm_first, w_qkv, w_feature, w_out, norm_second, w_up, w_down, cotangent
):
    wqkv=jnp.transpose(w_qkv,(1,0,2))
    residual_in = tokens[0].astype(jnp.float32)
    normed_first, first_back = jax.vjp(normalize, residual_in, norm_first)
    first_low = normed_first.astype(jnp.bfloat16)
    first_rows = lax.all_gather(first_low, "head", axis=0, tiled=True)
    cot_low = cotangent[0]
    cot_rows = lax.all_gather(cot_low, "hidden", axis=0, tiled=True)
    proj,feat,mixed,rden,part=fwd(lengths,first_rows,wqkv,w_feature,w_out)
    branch = lax.psum_scatter(part, "head", scatter_dimension=0, tiled=True).astype(jnp.float32)
    middle = residual_in + branch
    normed_second, second_back = jax.vjp(normalize, middle, norm_second)
    second_low = normed_second.astype(jnp.bfloat16)
    second_rows = lax.all_gather(second_low, "hidden", axis=0, tiled=True)
    hidden_pre = jnp.dot(second_rows, w_up, preferred_element_type=jnp.float32)
    active = smooth_gate(hidden_pre).astype(jnp.bfloat16)
    gate_grad = jax.vjp(smooth_gate, hidden_pre)[1]
    d_active = jnp.einsum("nd,fd->nf", cot_rows, w_down, preferred_element_type=jnp.float32)
    d_pre = gate_grad(d_active)[0].astype(jnp.bfloat16)
    d_second = lax.psum_scatter(
        jnp.einsum("nf,df->nd", d_pre, w_up, preferred_element_type=jnp.float32).astype(jnp.bfloat16),
        "hidden",
        scatter_dimension=0,
        tiled=True,
    ).astype(jnp.float32)
    mlp_result = lax.psum_scatter(
        jnp.dot(active, w_down, preferred_element_type=jnp.float32).astype(jnp.bfloat16),
        "hidden",
        scatter_dimension=0,
        tiled=True,
    ).astype(jnp.float32)
    block_out = (middle + mlp_result).astype(jnp.bfloat16)
    grad_down = jnp.einsum("nf,nd->fd", active, cot_rows, preferred_element_type=jnp.float32)
    grad_up = jnp.einsum("nd,nf->df", second_rows, d_pre, preferred_element_type=jnp.float32)
    d_middle_norm, grad_norm_second = second_back(d_second)
    d_middle = cot_low.astype(jnp.float32) + d_middle_norm
    d_branch_rows = lax.all_gather(d_middle.astype(jnp.bfloat16), "head", axis=0, tiled=True)
    gq,grad_feature,go,dfirst=bwd(first_rows,wqkv,w_feature,w_out,proj,feat,mixed,rden,d_branch_rows)
    d_first = lax.psum_scatter(dfirst, "head", scatter_dimension=0, tiled=True).astype(jnp.float32)
    d_input_norm, grad_norm_first = first_back(d_first)
    grad_tokens = d_middle + d_input_norm
    grad_up, grad_down = (
        lax.psum(grad_up.astype(jnp.bfloat16), ("dp", "head")).astype(jnp.float32),
        lax.psum(grad_down.astype(jnp.bfloat16), ("dp", "head")).astype(jnp.float32),
    )
    gq, grad_feature, go = (
        lax.psum(gq, ("dp", "hidden")).astype(jnp.float32),
        lax.psum(grad_feature.astype(jnp.bfloat16), ("dp", "hidden")).astype(jnp.float32),
        lax.psum(go, ("dp", "hidden")).astype(jnp.float32),
    )
    grad_norm_first, grad_norm_second = lax.psum(
        (grad_norm_first, grad_norm_second), ("dp", "head", "hidden")
    )
    return (
        block_out[None],
        grad_tokens[None],
        grad_norm_first,
        jnp.transpose(gq,(1,0,2)),
        grad_feature,
        go,
        grad_norm_second,
        grad_up,
        grad_down,
    )


ORDER=("n0","w","t","n1","a","cy","pt","cz","po","w","cx","pa","sa","pb","sb","cy","tr","w","ya","xa","cz","xb","yb","w","bx","by","bo","ya","xb","bd","gu","Yb","gd","Xa","u","Da","Db","v","dno","dn","A!","Da","Db","fin","B!","u","dm","v","b","go","do","u","0","p0","B","p1","1","0","v","p2","0","3","A","2","1","p3","3","4","0","u","2","v","3","fo","0","1","4","fm","0","3","n","2","u","4","1","3","B","2","4","1","A","3","4","n","2","v","1","u","u","n","4","0","2","f","1","3","v","0","n","3","4","v","2","1","4","n","2")
EARLY_X=(3,)
SUM_ALL=()
GATHER_ALL=()
ROWS_X_FIRST=True

MESH=pl.DeviceIdType.MESH
ANY=pl.BlockSpec(memory_space=pl.ANY)
EPS=1e-05

def place():
    dp=lax.axis_index("dp")
    return dp//2, dp%2, lax.axis_index("head"), lax.axis_index("hidden")

def only(when,act):
    if when is None: act()
    else: pl.when(when)(act)

class Wires:
    def __init__(self,sems):
        self.sems=sems; self.count=0; self.all=[]
    def send(self,src,dst,dev,when=None):
        i=self.count
        self.count+=1
        k=pltpu.make_async_remote_copy(src_ref=src,dst_ref=dst,send_sem=self.sems.at[0,i],recv_sem=self.sems.at[1,i],device_id=dev,device_id_type=MESH)
        only(when,k.start)
        self.all.append((k,when))
        return k

def greet(peers):
    bar=pltpu.get_barrier_semaphore()
    for d in peers: pl.semaphore_signal(bar,inc=1,device_id=d,device_id_type=MESH)
    pl.semaphore_wait(bar,len(peers))

def unit(values):
    centred=values-jnp.mean(values,axis=-1,keepdims=True)
    r=lax.rsqrt(jnp.mean(centred*centred,axis=-1,keepdims=True)+EPS)
    return centred*r, r

def norm_back(values,grad,gain):
    xh,r=unit(values)
    e=grad*gain
    inner=e-jnp.mean(e,axis=-1,keepdims=True)-xh*jnp.mean(e*xh,axis=-1,keepdims=True)
    return r*inner, jnp.sum(grad*xh,axis=0,keepdims=True)

def gate(v):
    k=0.7978845608; a=0.044715
    sq=v*v
    t=jnp.tanh(k*v*(1.0+a*sq))
    half=0.5*(1.0+t)
    return v*half, half+0.5*v*(1.0-t*t)*(k+(3.0*a*k)*sq)

def add_into(dst,src,step):
    rows=dst.shape[0]
    def body(i,_):
        r=pl.ds(pl.multiple_of(i*step,step),step)
        dst[r]=(dst[r].astype(F32)+src[r].astype(F32)).astype(dst.dtype)
        return 0
    lax.fori_loop(0,rows//step,body,0)

def layer_kernel(len_ref,tok,cot,g1,g2,wqkv,wf,wout,wup,wdn,
                 bo_o,gt_o,go_o,gp_o,gu_o,gd_o,gn_o,
                 T,rows,rowsT,wq,wo,proj,feat,mixed,rden,own,snd,rcv,mid,
                 SA,CA,Wu,Wd,act,dpre,P,ML,gu,gd,cu,cd,zu,zd,mu,md,yu,yd,rx,ry,rdx,rdy,
                 dmid,db,datt,dproj,G0,GP,C0,CP,X0,XP,U0,UP,W0,WP,
                 ma,mb,na,nb,bo,dfs,dfr,gn2,gsum,gn,gr,w2,loc,sems):
    x,c,y,z=place()
    nh=lax.axis_size("hidden"); last=nh-1
    nx,ny,nc=((1-x)*2+c,y,z),(x*2+c,1-y,z),(x*2+1-c,y,z)
    low,side=z%2,z//2
    z1,z2=z+1-2*low,(z+2)%nh
    inner=low!=side
    mate=(x*2+c,y,last-z)
    n1,n2=(x*2+c,y,z1),(x*2+c,y,z2)
    R,d=tok.shape; n=2*R; H=R//2
    hd=wf.shape[-1]; w=2*hd; pairs=w2.shape[1]; f=wup.shape[1]; fs=f//4
    qo,qx,qy,qd=x*2+y,(1-x)*2+y,x*2+1-y,(1-x)*2+1-y
    mine=pl.ds(pl.multiple_of(y*R,R),R); other=pl.ds(pl.multiple_of((1-y)*R,R),R)
    A=pl.ds(0,H); B=pl.ds(H,H)
    half=lambda size,b: pl.ds(pl.multiple_of(b*size,size),size)
    hu,hw=d//2,fs//2
    uo,ua,vo,va=half(hu,c),half(hu,1-c),half(hw,c),half(hw,1-c)
    at=lambda q: pl.ds(pl.multiple_of(q*fs,fs),fs)
    nloc=[0]; pend=[]; seen=[]
    def lc(s,t,out=False):
        k=pltpu.make_async_copy(s,t,loc.at[nloc[0]]); nloc[0]+=1
        k.start()
        if out: pend.append(k)
        return k
    wires=Wires(sems)
    send=wires.send
    l_tok=lc(tok,T.at[mine])
    l_wq=[lc(wqkv.at[i],wq.at[i]) for i in range(3)]
    greet((nx,ny,nc)+tuple((x*2+c,y,(z+t)%nh) for t in range(1,nh)))

    def simple(src,dst,dev):
        k=send(src,dst,dev)
        yield
        k.wait_recv()

    def onward(src,dst,dev,src2,dst2,dev2,between=None):
        k=send(src,dst,dev)
        yield
        k.wait_recv()
        if between is not None: between()
        k=send(src2,dst2,dev2)
        yield
        k.wait_recv()

    def weights():
        wdh=lambda q: pl.ds(pl.multiple_of(q*fs+c*hw,hw),hw)
        wdo=lambda q: pl.ds(pl.multiple_of(q*fs+(1-c)*hw,hw),hw)
        for s in range(1,nh):
            now=[]
            for right in (True,False):
                j=(z-s+1) if right else (z+s-1)
                when=((z<last)&(j>=0)) if right else ((z>0)&(j<=last))
                jj=jnp.clip(j,0,last)
                dev=(x*2+c,y,jnp.clip(z+1 if right else z-1,0,last))
                if s==1: su,sd=wup.at[uo,at(qo)],wdn.at[wdh(qo)]
                else: su,sd=Wu.at[uo,at(jj)],Wd.at[wdh(jj)]
                got=(z-s>=0) if right else (z+s<=last)
                now.append((send(su,Wu.at[uo,at(jj)],dev,when),send(sd,Wd.at[wdh(jj)],dev,when),got))
            yield
            for a,b,got in now: only(got,a.wait_recv); only(got,b.wait_recv)
            for right,(_,_,got) in zip((True,False),now):
                jj=jnp.clip((z-s) if right else (z+s),0,last)
                shared.append((send(Wu.at[uo,at(jj)],Wu.at[uo,at(jj)],nc,got),got))
                shared.append((send(Wd.at[wdh(jj)],Wd.at[wdh(jj)],nc,got),got))
        yield
        for k,got in shared: only(got,k.wait_recv)
    shared=[]

    def grads(G,bufs,O,early,sum_all,gather_all):
        steps=[(nc,c),(nx,x),(n1,low),(n2,side)]
        size=G.shape[0]; base=0
        for i in range(2 if sum_all else 4):
            dev,bit=steps[i]
            size//=2
            away=pl.multiple_of(base+(1-bit)*size,16)
            base=pl.multiple_of(base+bit*size,16)
            k=send(G.at[pl.ds(away,size)],bufs[i],dev)
            yield
            k.wait_recv()
            add_into(G.at[pl.ds(base,size)],bufs[i],size//2 if size%32==0 else size)
        if sum_all:
            size//=4
            slots=[bufs[2].at[pl.ds(0,size)],bufs[2].at[pl.ds(size,size)],bufs[3]]
            ks=[]
            for t in (2,1,3):
                j=(z+t)%nh
                piece=pl.ds(pl.multiple_of(base+(2*(j%2)+j//2)*size,16),size)
                ks.append(send(G.at[piece],slots[t-1],(x*2+c,y,j)))
            yield
            base=pl.multiple_of(base+(2*low+side)*size,16)
            for k in ks: k.wait_recv()
            for s in slots: add_into(G.at[pl.ds(base,size)],s,size)
        src=G.at[pl.ds(base,size)]
        place_=[c,x,low,side]
        copy=lc(src,O.at[tuple(place_)])
        def gather(devs,*dims):
            nonlocal src,copy
            ks=[send(O.at[tuple(place_)] if src is None else src,O.at[tuple(place_)],dev) for dev in devs]
            src=None
            yield
            for k in ks: k.wait_recv()
            if copy is not None: copy.wait()
            copy=None
            for i in dims: place_[i]=slice(None)
        if early: yield from gather([nx],1)
        if gather_all: yield from gather([(x*2+c,y,(z+t)%nh) for t in (2,1,3)],2,3)
        else:
            yield from gather([n2],3)
            yield from gather([n1],2)
        if not early: yield from gather([nx],1)
        yield from gather([nc],0)

    def mlp_grads(W,kept,away,core,far,middle,final,whole,piece,step):
        two=lambda i: pl.ds(pl.multiple_of(2*i,2),2)
        k=send(W.at[:,away],core,nc)
        yield
        k.wait_recv()
        for j in range(nh): add_into(W.at[j,kept],core.at[j],step)
        k=send(W.at[two(1-low),kept],far,n1)
        yield
        k.wait_recv()
        for j in range(2): add_into(W.at[2*low+j,kept],far.at[j],step)
        m=send(W.at[two(low),kept],middle,mate,inner)
        yield
        def take():
            m.wait_recv()
            k.wait_send()
            for j in range(2): W[2*side+j,kept]=middle[j]
        pl.when(inner)(take)
        seen.append(k)
        k2=send(W.at[2*side+1-low,kept],final,n1)
        yield
        k2.wait_recv()
        add_into(W.at[z,kept],final,step)
        l=lc(W.at[z,kept],piece(qo))
        k=send(W.at[z,kept],piece(qo),nx)
        k2=send(W.at[z,kept],piece(qo),ny)
        yield
        k.wait_recv()
        k=send(piece(qx),piece(qx),ny)
        yield
        k.wait_recv(); k2.wait_recv(); l.wait()
        k=send(whole,whole,nc)
        yield
        k.wait_recv()

    def mlp_rows(r,near,dev,q1,q2,buf,far,q3):
        k=[send(ML.at[q1,r],buf.at[0],near),send(ML.at[q2,r],buf.at[1],near)]
        yield
        for t in k: t.wait_recv()
        add_into(ML.at[qo,r],buf.at[0],H); add_into(ML.at[q3,r],buf.at[1],H)
        k=send(ML.at[q3,r],far,dev)
        yield
        k.wait_recv()
        bo[r]=(mid[r]+(ML[qo,r].astype(F32)+far[...].astype(F32))).astype(BF)
        lc(bo.at[r],bo_o.at[r],True)

    def first_grad(r):
        t=mm_nt(dproj[0,r],wq[0])+mm_nt(dproj[1,r],wq[1])
        return t+mm_nt(dproj[2,r],wq[2])

    def first_rows():
        t=first_grad(other)
        dfs[...]=t.astype(BF)
        k=send(dfs,dfr,ny)
        xo,_=unit(T[other].astype(F32))
        gsum[...]=jnp.sum(t*xo,axis=0,keepdims=True)
        yield
        k.wait_recv()
        dx,_=norm_back(T[mine].astype(F32),own[...]+dfr[...].astype(F32),g1[...])
        dmid[...]=dmid[...]+dx
        lc(dmid,gt_o,True)

    def gains():
        t=first_grad(mine)
        own[...]=t
        xm,_=unit(T[mine].astype(F32))
        gn[...]=jnp.zeros_like(gn)
        gn[0,0:1]=gsum[...]+jnp.sum(t*xm,axis=0,keepdims=True)
        gn[0,1:2]=gn2[...]
        order=[nc,nx,ny,n1,n2]
        for i,dev in enumerate(order):
            k=send(gn.at[i],gr.at[i],dev)
            yield
            k.wait_recv()
            gn[i+1]=gn[i]+gr[i]
        gn_o[...]=gn[len(order)]

    def sum_a(): P[qy,A]=(P[qy,A].astype(F32)+rdx[...].astype(F32)).astype(BF)
    def sum_b(): P[qx,B]=(P[qx,B].astype(F32)+rdy[...].astype(F32)).astype(BF)
    S_=lambda q,r: SA.at[q,r]
    chains={
        "t":simple(tok,T.at[mine],ny),
        "w":weights(),
        "cx":simple(cot,CA.at[qo],nx),
        "cy":onward(cot.at[A],CA.at[qo,A],ny,CA.at[qy,A],CA.at[qy,A],nx),
        "cz":onward(cot.at[B],CA.at[qo,B],ny,CA.at[qy,B],CA.at[qy,B],nx),
        "pa":simple(snd.at[A],rcv.at[A],ny),
        "pb":simple(snd.at[B],rcv.at[B],ny),
        "xa":simple(S_(qo,A),S_(qo,A),nx),
        "yb":simple(S_(qo,B),S_(qo,B),ny),
        "xb":onward(S_(qo,B),S_(qo,B),nx,S_(qx,B),S_(qx,B),ny),
        "ya":onward(S_(qo,A),S_(qo,A),ny,S_(qy,A),S_(qy,A),nx),
        "Xa":simple(P.at[qx,A],rx.at[A],nx),
        "Yb":simple(P.at[qy,B],ry.at[B],ny),
        "Da":onward(P.at[qd,A],rdx,nx,P.at[qy,A],ry.at[A],ny,sum_a),
        "Db":onward(P.at[qd,B],rdy,ny,P.at[qx,B],rx.at[B],nx,sum_b),
        "b":simple(db.at[mine],db.at[mine],ny),
        "u":mlp_grads(gu,uo,ua,cu,zu,mu,yu,gu_o.at[uo],lambda q: gu_o.at[uo,at(q)],64),
        "v":mlp_grads(gd,vo,va,cd,zd,md,yd,gd_o.at[:,vo],lambda q: gd_o.at[q,vo],16),
        "A":mlp_rows(A,nx,ny,qx,qd,ma,na,qy),"B":mlp_rows(B,nx,ny,qx,qd,mb,nb,qy) if ROWS_X_FIRST else mlp_rows(B,ny,nx,qy,qd,mb,nb,qx),
        "f":first_rows(),"n":gains(),
        "0":grads(G0,(C0,X0,U0,W0),go_o,-1 in EARLY_X,-1 in SUM_ALL,-1 in GATHER_ALL)}
    for p in range(pairs): chains[str(p+1)]=grads(GP.at[p],(CP.at[p],XP.at[p],UP.at[p],WP.at[p]),gp_o.at[p],p in EARLY_X,p in SUM_ALL,p in GATHER_ALL)
    turns={name:-1 for name in chains}
    def go(*names):
        for name in names:
            next(chains[name],None)
            turns[name]+=1
    def need(**steps):
        for name,count in steps.items():
            while turns[name]<count: go(name)

    ones=half_ones(2*w,hd); ones1=half_ones(w,hd)
    valid=lax.broadcasted_iota(jnp.int32,(n,2*w),0)<len_ref[0,0]
    def first(r):
        xh,_=unit(T[r].astype(F32))
        rows[r]=(xh*g1[...]).astype(BF)
    def project(r):
        for i in range(3): proj[i,r]=mm(rows[r],wq[i]).astype(BF)
    def heads(p,_):
        cc=pl.ds(pl.multiple_of(p*w,w),w)
        fq=features(proj[0,:,cc],w2[0,p],ones,hd).astype(BF)
        fk=jnp.where(valid,features(proj[1,:,cc],w2[1,p],ones,hd),0.0).astype(BF)
        feat[0,p]=fq; feat[1,p]=fk
        m,rd=attend(fq,fk,proj[2,:,cc],hd)
        mixed[:,cc]=m.astype(BF); rden[:,cc]=rd
        return 0
    def second(start):
        r=pl.ds(start,H)
        middle=T[pl.ds(pl.multiple_of(y*R+start,H),H)].astype(F32)+(own[r]+rcv[r].astype(F32))
        mid[r]=middle
        xh,_=unit(middle)
        SA[qo,r]=(xh*g2[...]).astype(BF)
    def block(qi,keep):
        need(w=nh)
        while l_own: l_own.pop().wait()
        a,ga=gate(mm(SA[qi],Wu[...]))
        act[qi]=a.astype(BF)
        dp=(mm_nt(CA[qi],Wd[...])*ga).astype(BF)
        dpre[qi]=dp
        d2=mm_nt(dp,Wu[...])
        if keep: own[...]=d2
        else: P[qi]=d2.astype(BF)
    def down(qi): ML[qi]=mm(act[qi],Wd[...]).astype(BF)
    def pair(p):
        cc=slice(p*w,(p+1)*w)
        fq=feat[0,p]; fk=feat[1,p]
        dfq,dfk,dv=attend_back(fq,fk,proj[2,:,cc],mixed[:,cc],rden[:,cc],datt[:,cc],ones1,hd)
        parts=[]
        for t,(ft,df) in enumerate(((fq,dfq),(fk,dfk))):
            du=feature_back(ft,df,ones)
            GP[p,pl.ds(3*d+t*w,w)]=mm_tn(proj[t,:,cc],du).astype(BF)
            parts.append(mm_nt(du,w2[t,p]).astype(BF))
        parts.append(dv.astype(BF))
        for t in range(3): dproj[t,:,cc]=parts[t]
        g=mm(rowsT[...],jnp.concatenate(parts,axis=1)).astype(BF)
        for t in range(3): GP[p,pl.ds(t*d,d)]=g[:,t*w:(t+1)*w]
    def do(name):
        if name=="n0":
            pair_weights(wf,w2)
            l_tok.wait()
            first(mine)
            for k in l_wq: k.wait()
            project(mine)
        elif name=="n1":
            need(t=1)
            first(other); project(other)
        elif name=="a": lax.fori_loop(0,pairs,heads,0)
        elif name=="pt":
            l_wo.wait()
            snd[...]=mm(mixed[other],wo[...]).astype(BF)
            go("pa","pb")
        elif name=="po": own[...]=mm(mixed[mine],wo[...])
        elif name=="tr": rowsT[...]=rows[...].T
        elif name=="sa": need(pa=1); second(0); go("xa","ya")
        elif name=="sb": need(pb=1); second(H); go("xb","yb")
        elif name=="bo":
            block(qo,True)
        elif name=="dno": down(qo)
        elif name=="bx":
            need(xa=1,xb=1,cx=1)
            block(qx,False); go("Xa")
        elif name=="by":
            need(ya=1,yb=1,cy=1,cz=1)
            block(qy,False); go("Yb")
        elif name=="bd":
            need(xb=2,ya=2,cy=2,cz=2)
            block(qd,False); go("Da","Db")
        elif name=="gu":
            sa=SA[...].reshape(4*R,d)
            for j in range(nh//2):
                t=mm_tn(sa,dpre[:,:,pl.ds(2*j*fs,2*fs)].reshape(4*R,2*fs)).astype(BF)
                gu[2*j]=t[:,:fs]; gu[2*j+1]=t[:,fs:]
            go("u")
        elif name=="dn":
            for q in (qx,qy,qd): down(q)
        elif name=="gd":
            ca=CA[...].reshape(4*R,d)
            for j in range(nh): gd[j]=mm_tn(act[:,:,pl.ds(j*fs,fs)].reshape(4*R,fs),ca).astype(BF)
            go("v")
        elif name=="A!": go("A")
        elif name=="B!": go("B")
        elif name=="fin":
            need(Da=2,Db=2,Xa=1,Yb=1)
            dx,g=norm_back(mid[...],own[...]+(rx[...].astype(F32)+ry[...].astype(F32)),g2[...])
            gn2[...]=g
            dm=CA[qo].astype(F32)+dx
            dmid[...]=dm
            db[mine]=dm.astype(BF)
            go("b")
        elif name=="dm": datt[mine]=mm_nt(db[mine],wo[...])
        elif name=="do":
            need(b=1)
            datt[other]=mm_nt(db[other],wo[...])
        elif name=="go":
            G0[...]=mm_tn(mixed[...],db[...]).astype(BF)
            go("0")
        elif name[0]=="p" and len(name)==2 and name[1].isdigit():
            p=int(name[1])
            if p<pairs: pair(p); go(str(p+1))
        elif name=="fo": go("f")
        elif name=="fm": go("n")
        elif name in chains: go(name)
    go("t","cy","cz","cx","w")
    l_wo=lc(wout,wo)
    l_own=[lc(wup.at[:,at(qo)],Wu.at[:,at(z)]),lc(wdn.at[at(qo)],Wd.at[at(z)]),lc(cot,CA.at[qo])]
    for name in ORDER: do(name)
    for name in chains:
        for _ in chains[name]: pass
    outer=jnp.logical_not(inner)
    for k,when in wires.all: only(outer if any(k is t for t in seen) else when,k.wait_send)
    for k in pend: k.wait()

def layer(length,tok,cot,g1,g2,wqkv,wf,wout,wup,wdn):
    R,d=tok.shape; n=2*R; H=R//2; c=wout.shape[0]; h=wf.shape[1]; hd=wf.shape[-1]; pairs=h//2; w=2*hd; q=3*d+2*w
    f=wup.shape[1]; fs=f//4; nz=lax.axis_size("hidden")
    D=pltpu.SemaphoreType.DMA
    b=lambda *s: pltpu.VMEM(s,BF)
    e=lambda *s: pltpu.VMEM(s,F32)
    return pl.pallas_call(layer_kernel,
      out_shape=(S((R,d),BF),S((R,d),F32),S((2,2,2,2,c//16,d),BF),S((pairs,2,2,2,2,q//16,w),BF),S((d,f),BF),S((4,fs,d),BF),S((8,d),F32)),
      in_specs=[SM,ANY,ANY,VM,VM,ANY,VM,ANY,ANY,ANY],
      out_specs=[ANY]*6+[VM],
      scratch_shapes=[b(n,d),b(n,d),b(d,n),b(3,d,c),b(c,d),b(3,n,c),b(2,pairs,n,2*w),b(n,c),e(n,c),e(R,d),b(R,d),b(R,d),e(R,d),
        b(4,R,d),b(4,R,d),b(d,f),b(f,d),b(4,R,f),b(4,R,f),b(4,R,d),b(4,R,d),b(nz,d,fs),b(nz,fs,d),b(nz,d//2,fs),b(nz,fs//2,d),
        b(2,d//2,fs),b(2,fs//2,d),b(2,d//2,fs),b(2,fs//2,d),b(d//2,fs),b(fs//2,d),b(R,d),b(R,d),b(H,d),b(H,d),
        e(R,d),b(n,d),e(n,c),b(3,n,c),b(c,d),b(pairs,q,w),b(c//2,d),b(pairs,q//2,w),b(c//4,d),b(pairs,q//4,w),
        b(c//8,d),b(pairs,q//8,w),b(c//16,d),b(pairs,q//16,w),
        b(2,H,d),b(2,H,d),b(H,d),b(H,d),b(R,d),b(R,d),b(R,d),e(1,d),e(1,d),e(6,8,d),e(5,8,d),
        b(2,pairs,w,w),D((24,)),D((2,128))],
      compiler_params=pltpu.CompilerParams(vmem_limit_bytes=63*2**20,collective_id=1,has_side_effects=True),
      cost_estimate=pl.CostEstimate(flops=24*10**9,bytes_accessed=40*10**6,transcendentals=2*10**6))(
      length,tok,cot,g1,g2,wqkv,wf,wout,wup,wdn)

def per_device_k1(
    tokens, lengths, norm_first, w_qkv, w_feature, w_out, norm_second, w_up, w_down, cotangent
):
    h,hd=w_feature.shape[1],w_feature.shape[3]; w=2*hd
    block_out,grad_tokens,go,gp,gu,gd,gn=layer(lengths,tokens[0],cotangent[0],norm_first[None],norm_second[None],jnp.transpose(w_qkv,(1,0,2)),w_feature,w_out,w_up,w_down)
    go=go.reshape(w_out.shape); gp=gp.reshape(h//2,-1,w)
    go,gq,gf,gu,gd,block_out,grad_tokens,n1,n2=finish(go,gp,gu,gd.reshape(gd.shape[0]*gd.shape[1],-1),block_out,grad_tokens,gn,hd)
    return (
        block_out[None],
        grad_tokens[None],
        n1[0],
        jnp.transpose(gq,(1,0,2)),
        gf,
        go,
        n2[0],
        gu,
        gd,
    )

def finish_kernel(go,g0,g1,g2,gf,gu,gd,bo,gt,gn,go_o,gq_o,gf_o,gu_o,gd_o,bo_o,gt_o,n1_o,n2_o):
    for a,b in ((go,go_o),(gu,gu_o),(gd,gd_o)): b[...]=a[...].astype(F32)
    bo_o[...]=bo[...]
    gt_o[...]=gt[...]
    pairs,_,w=g0.shape; hd=w//2
    for t,g in enumerate((g0,g1,g2)):
        for p in range(pairs): gq_o[t,:,p*w:(p+1)*w]=g[p].astype(F32)
    @pl.when(pl.program_id(0)==0)
    def _():
        n1_o[...]=gn[0:1]; n2_o[...]=gn[1:2]
        for t in range(2):
            for p in range(pairs):
                for s in range(2):
                    gf_o[t,2*p+s]=gf[p,t*w+s*hd:t*w+(s+1)*hd,s*hd:(s+1)*hd].astype(F32)

def finish(go,gp,gu,gd,bo,gt,gn,hd,N=2):
    c,d=go.shape; pairs,_,w=gp.shape; f=gu.shape[1]
    B=pl.BlockSpec
    row=lambda a: B((a.shape[0]//N,a.shape[1]),lambda i:(i,0))
    all_=lambda a: B(a.shape,lambda i:(0,)*len(a.shape))
    part=lambda t: B((pairs,d//N,w),lambda i:(0,i+N*t,0))
    gf=S((2,2*pairs,hd,hd),F32); n=S((1,d),F32)
    return pl.pallas_call(finish_kernel,grid=(N,),
      out_shape=(S((c,d),F32),S((3,d,c),F32),gf,S((d,f),F32),S((f,d),F32),S(bo.shape,BF),S(gt.shape,F32),n,n),
      in_specs=[row(go),part(0),part(1),part(2),B((pairs,2*w,w),lambda i:(0,3*d//(2*w),0)),row(gu),row(gd),row(bo),row(gt),all_(gn)],
      out_specs=[row(go),B((3,d//N,c),lambda i:(0,i,0)),all_(gf),row(gu),row(gd),row(bo),row(gt),all_(n),all_(n)],
      compiler_params=pltpu.CompilerParams(vmem_limit_bytes=62*2**20))(go,gp,gp,gp,gp,gu,gd,bo,gt,gn)


def solution(mesh):
    in_specs = (
        P(("dp", "hidden"), "head", None),
        P(("dp", "hidden"), None),
        P(),
        P(None, None, "head"),
        P(None, "head", None, None),
        P("head", None),
        P(),
        P(None, "hidden"),
        P("hidden", None),
        P(("dp", "hidden"), "head", None),
    )
    out_specs = (
        P(("dp", "hidden"), "head", None),
        P(("dp", "hidden"), "head", None),
        P(),
        P(None, None, "head"),
        P(None, "head", None, None),
        P("head", None),
        P(),
        P(None, "hidden"),
        P("hidden", None),
    )
    near=dict(mesh.shape)=={"dp":4,"head":2,"hidden":4}
    return jax.shard_map(
        per_device_k1 if near else per_device, mesh=mesh, in_specs=in_specs, out_specs=out_specs, check_vma=False
    )
```

profile of v0, /device:TPU:0, one launch (start us, length us, event | category | flops | bytes accessed | tf_op | source)
XLA Modules:
  0.0 174.3 jit_solution(2894071625091234314)
XLA Ops:
  1.3 162.7 %shard_map.169 = (bf16[256,1024]{1,0:T(8,128)(2,1)}, f32[256,1024]{1,0:T(8,128)}, bf16[2,2,2,2,32,1024]{5,4,3,2,1,0:T(8,128)(2,1)}, bf16[4,2,2,2,2,208,128]{6,5,...) custom-call(s32[1,1]{1,0:T(1,128)S(6)} %copy.19.len_ref, ...), custom_call_target="tpu_custom_call" | custom-call | flops 24000000000 | bytes 40000000 | tf_op jit(solution)/shard_map/pallas_call | solution.py:669
  164.0 9.8 %shard_map.170 = (f32[512,1024]{1,0:T(8,128)}, f32[3,1024,512]{2,1,0:T(8,128)}, f32[2,8,64,64]{3,2,1,0:T(8,128)}, f32[1024,1024]{1,0:T(8,128)}, f32[1024,1024]{1...) custom-call(bf16[512,1024]{1,0:T(8,128)(2,1)} %bitcast.18, ...), custom_call_target="tpu_custom_call" | custom-call | tf_op jit(solution)/shard_map/pallas_call | solution.py:725
where the time goes:
time: 178 us; the launch traced here: 174 us
  Pallas kernels  173 us (97%)
    pallas_call x1, Pallas kernels, layer(): pl.pallas_call(layer_kernel, out_shape=(S((R, d), BF), S((R, d), F32), S(...  163 us
    pallas_call x1, Pallas kernels, finish(): pl.pallas_call(finish_kernel, grid=(N,), out_shape=(S((c, d), F32), S((3,...  9.85 us

commit v1 on v0

--- a/solution.py
+++ b/solution.py
@@ -251,7 +251,7 @@
     )
 
 
-ORDER=("n0","w","t","n1","a","cy","pt","cz","po","w","cx","pa","sa","pb","sb","cy","tr","w","ya","xa","cz","xb","yb","w","bx","by","bo","ya","xb","bd","gu","Yb","gd","Xa","u","Da","Db","v","dno","dn","A!","Da","Db","fin","B!","u","dm","v","b","go","do","u","0","p0","B","p1","1","0","v","p2","0","3","A","2","1","p3","3","4","0","u","2","v","3","fo","0","1","4","fm","0","3","n","2","u","4","1","3","B","2","4","1","A","3","4","n","2","v","1","u","u","n","4","0","2","f","1","3","v","0","n","3","4","v","2","1","4","n","2")
+ORDER=("n0","w","t","n1","a","cy","pt","po","cz","w","pa","sa","cy","tr","pb","sb","w","w","xa","ya","cz","xb","cx","yb","bx","by","ya","bo","xb","bd","gu","gd","u","Yb","Db","Da","dno","Dc","Dd","dn","A!","Da","Xa","Dd","v","Dc","fi","u","B!","Db","fj","dm","v","b","d","go","u","0","do","p0","p1","0","1","2","u","v","A","p2","0","1","p3","2","fo","4","0","1","fm","2","3","0","1","4","v","3","2","f","u","4","3","0","v","2","1","4","u","n","3","B","2","4","0","1","n","3","A","n","4","3","B","2","1","v","0","n","2","v","u","4","1","3","4","n","3")
 EARLY_X=(3,)
 SUM_ALL=()
 GATHER_ALL=()
@@ -330,6 +330,7 @@
     qo,qx,qy,qd=x*2+y,(1-x)*2+y,x*2+1-y,(1-x)*2+1-y
     mine=pl.ds(pl.multiple_of(y*R,R),R); other=pl.ds(pl.multiple_of((1-y)*R,R),R)
     A=pl.ds(0,H); B=pl.ds(H,H)
+    top,end=(pl.ds(pl.multiple_of(y*R+i*H,H),H) for i in range(2))
     half=lambda size,b: pl.ds(pl.multiple_of(b*size,size),size)
     hu,hw=d//2,fs//2
     uo,ua,vo,va=half(hu,c),half(hu,1-c),half(hw,c),half(hw,1-c)
@@ -504,8 +505,13 @@
             gn[i+1]=gn[i]+gr[i]
         gn_o[...]=gn[len(order)]
 
-    def sum_a(): P[qy,A]=(P[qy,A].astype(F32)+rdx[...].astype(F32)).astype(BF)
-    def sum_b(): P[qx,B]=(P[qx,B].astype(F32)+rdy[...].astype(F32)).astype(BF)
+    Q=H//2
+    quarters=[pl.ds(i*Q,Q) for i in range(4)]
+    def diagonal(i):
+        r=quarters[i]; s=pl.ds((i%2)*Q,Q)
+        near,q,buf,out,far=(nx,qy,rdx,ry,ny) if i<2 else (ny,qx,rdy,rx,nx)
+        def add(): P[q,r]=(P[q,r].astype(F32)+buf[s].astype(F32)).astype(BF)
+        return onward(P.at[qd,r],buf.at[s],near,P.at[q,r],out.at[r],far,add)
     S_=lambda q,r: SA.at[q,r]
     chains={
         "t":simple(tok,T.at[mine],ny),
@@ -521,9 +527,9 @@
         "ya":onward(S_(qo,A),S_(qo,A),ny,S_(qy,A),S_(qy,A),nx),
         "Xa":simple(P.at[qx,A],rx.at[A],nx),
         "Yb":simple(P.at[qy,B],ry.at[B],ny),
-        "Da":onward(P.at[qd,A],rdx,nx,P.at[qy,A],ry.at[A],ny,sum_a),
-        "Db":onward(P.at[qd,B],rdy,ny,P.at[qx,B],rx.at[B],nx,sum_b),
-        "b":simple(db.at[mine],db.at[mine],ny),
+        "Da":diagonal(0),"Dc":diagonal(1),"Db":diagonal(2),"Dd":diagonal(3),
+        "b":simple(db.at[top],db.at[top],ny),
+        "d":simple(db.at[end],db.at[end],ny),
         "u":mlp_grads(gu,uo,ua,cu,zu,mu,yu,gu_o.at[uo],lambda q: gu_o.at[uo,at(q)],64),
         "v":mlp_grads(gd,vo,va,cd,zd,md,yd,gd_o.at[:,vo],lambda q: gd_o.at[q,vo],16),
         "A":mlp_rows(A,nx,ny,qx,qd,ma,na,qy),"B":mlp_rows(B,nx,ny,qx,qd,mb,nb,qy) if ROWS_X_FIRST else mlp_rows(B,ny,nx,qy,qd,mb,nb,qx),
@@ -570,6 +576,12 @@
         d2=mm_nt(dp,Wu[...])
         if keep: own[...]=d2
         else: P[qi]=d2.astype(BF)
+    def middle_grad(r,there):
+        dx,g=norm_back(mid[r],own[r]+(rx[r].astype(F32)+ry[r].astype(F32)),g2[...])
+        dm=CA[qo,r].astype(F32)+dx
+        dmid[r]=dm
+        db[there]=dm.astype(BF)
+        return g
     def down(qi): ML[qi]=mm(act[qi],Wd[...]).astype(BF)
     def pair(p):
         cc=slice(p*w,(p+1)*w)
@@ -614,7 +626,7 @@
             block(qy,False); go("Yb")
         elif name=="bd":
             need(xb=2,ya=2,cy=2,cz=2)
-            block(qd,False); go("Da","Db")
+            block(qd,False); go("Da","Db","Dc","Dd")
         elif name=="gu":
             sa=SA[...].reshape(4*R,d)
             for j in range(nh//2):
@@ -629,17 +641,17 @@
             go("v")
         elif name=="A!": go("A")
         elif name=="B!": go("B")
-        elif name=="fin":
-            need(Da=2,Db=2,Xa=1,Yb=1)
-            dx,g=norm_back(mid[...],own[...]+(rx[...].astype(F32)+ry[...].astype(F32)),g2[...])
-            gn2[...]=g
-            dm=CA[qo].astype(F32)+dx
-            dmid[...]=dm
-            db[mine]=dm.astype(BF)
+        elif name=="fi":
+            need(Da=2,Dc=2,Xa=1)
+            gn2[...]=middle_grad(A,top)
             go("b")
+        elif name=="fj":
+            need(Db=2,Dd=2,Yb=1)
+            gn2[...]=gn2[...]+middle_grad(B,end)
+            go("d")
         elif name=="dm": datt[mine]=mm_nt(db[mine],wo[...])
         elif name=="do":
-            need(b=1)
+            need(b=1,d=1)
             datt[other]=mm_nt(db[other],wo[...])
         elif name=="go":
             G0[...]=mm_tn(mixed[...],db[...]).astype(BF)

time: 178 us -> 177 us (level)
  the two profiles are of different devices: /device:TPU:0 before, /device:TPU:3 now
where the time goes in v1:
time: 177 us; the launch traced here: 174 us
  Pallas kernels  172 us (97%)
    pallas_call x1, Pallas kernels, layer(): pl.pallas_call(layer_kernel, out_shape=(S((R, d), BF), S((R, d), F32), S(...  162 us
    pallas_call x1, Pallas kernels, finish(): pl.pallas_call(finish_kernel, grid=(N,), out_shape=(S((c, d), F32), S((3,...  9.85 us

profile of v1, /device:TPU:3, one launch (start us, length us, event | category | flops | bytes accessed | tf_op | source)
XLA Modules:
  0.0 173.8 jit_solution(10265854669745785692)
XLA Ops:
  1.3 162.2 %shard_map.169 = (bf16[256,1024]{1,0:T(8,128)(2,1)}, f32[256,1024]{1,0:T(8,128)}, bf16[2,2,2,2,32,1024]{5,4,3,2,1,0:T(8,128)(2,1)}, bf16[4,2,2,2,2,208,128]{6,5,...) custom-call(s32[1,1]{1,0:T(1,128)S(6)} %copy.19.len_ref, ...), custom_call_target="tpu_custom_call" | custom-call | flops 24000000000 | bytes 40000000 | tf_op jit(solution)/shard_map/pallas_call | solution.py:681
  163.5 9.8 %shard_map.170 = (f32[512,1024]{1,0:T(8,128)}, f32[3,1024,512]{2,1,0:T(8,128)}, f32[2,8,64,64]{3,2,1,0:T(8,128)}, f32[1024,1024]{1,0:T(8,128)}, f32[1024,1024]{1...) custom-call(bf16[512,1024]{1,0:T(8,128)(2,1)} %bitcast.18, ...), custom_call_target="tpu_custom_call" | custom-call | tf_op jit(solution)/shard_map/pallas_call | solution.py:737
